TPU v7x, 256 devices: a whole 4x4x8 slice. The times are simulated.
256 devices in a mesh: row: 8 (over y, z_hi), col: 32 (over x, z_lo, core).
Axes of the slice: x: 4, y: 4, z: 8 (z_hi: 2, z_lo: 4; z = z_hi * 4 + z_lo), core: 2. Of those that a mesh axis runs over, the one named last changes fastest.
Arguments:
- a_values: bfloat16 [2, 12288, 4096], P(None, 'row', 'col'), may hold values from -0.44140625 to 0.44140625
- a_pattern: int32 [2, 96, 32], P(None, 'row', 'col'), may hold values 0 or 1
- c_mask: int32 [96, 96], P('row', 'col'), may hold values 0 or 1
Outputs:
- scores: float32 [12288, 12288], P('row', 'col')
All inputs are finite; a program needn't handle non-finite values. No bound on the sum of `a_pattern` or of `c_mask` on one device may be relied on, other than what follows from the above.
Results may differ from a plain program's by a relative error of at most 0.0003.
Values may be sent and summed in bfloat16 or wider, within the bound.
A program may use at most 128 MiB of HBM per device.

v0:
```python
import jax
import jax.numpy as jnp
from jax import lax
from jax.sharding import PartitionSpec as P

TILE = 128
SECTIONS = 2


def spread_tiles(pattern):
    grown = jnp.repeat(pattern, TILE, axis=-2)
    return jnp.repeat(grown, TILE, axis=-1)


def product_nt(left, right):
    return lax.dot_general(
        left, right, (((1,), (1,)), ((), ())), preferred_element_type=jnp.float32
    )


def shards(a_values, a_pattern, c_mask):
    live_tiles = a_values * spread_tiles(a_pattern).astype(jnp.bfloat16)
    row_count = live_tiles.shape[1]
    col_width = c_mask.shape[1] * TILE
    total = jnp.zeros((row_count, col_width), jnp.float32)
    for section in range(SECTIONS):
        local_panel = live_tiles[section]
        all_pages = lax.all_gather(local_panel, "row", axis=0, tiled=True)
        column_block = lax.all_to_all(all_pages, "col", split_axis=0, concat_axis=1, tiled=True)
        total = total + product_nt(
            lax.all_gather(local_panel, "col", axis=1, tiled=True), column_block
        )
    return total * spread_tiles(c_mask).astype(jnp.float32)


def solution(mesh):
    return jax.shard_map(
        shards,
        mesh=mesh,
        in_specs=(P(None, "row", "col"), P(None, "row", "col"), P("row", "col")),
        out_specs=P("row", "col"),
        check_vma=False,
    )
```

profile of v0, /device:TPU:1, one launch (start us, length us, event | category | flops | bytes accessed | tf_op | source)
XLA Modules:
  0.0 498.5 jit_solution(13141279547738618645)
XLA Ops:
  6.5 0.0 all-gather.15.cloned.1.call-start
  6.5 0.7 convert_element_type.22
  7.2 0.1 broadcast_bitcast_fusion.1
  7.3 1.6 broadcast_multiply_fusion
  8.9 1.0 fusion.10
  9.9 0.0 all-gather.15.cloned.1.call-update
  9.9 0.0 all-gather.11.cloned.1.call-start
  10.0 0.7 all-gather.11.cloned.1.call-update
  10.7 0.0 all-gather.13.cloned.1.call-start
  10.7 0.7 all-gather.13.cloned.1.call-update
  11.4 0.0 all-gather.9.cloned.1.call-start
  11.4 0.5 all-gather.9.cloned.1.call-update
  12.0 93.3 %all-gather.15.cloned.1.call-done = bf16[1,12288,128]{2,1,0:T(8,128)(2,1)} async-done(((bf16[1,1536,128]{2,1,0:T(8,128)(2,1)}), bf16[1,12288,128]{2,1,0:T(8,128)(2,1)}) %all-gather.15.cloned.1.call-update) | async-done | bytes 3145744 | tf_op jit(solution)/shard_map/all_gather | solution.py:28
  105.3 5.6 %all-to-all-start.1 = ((bf16[32,384,128]{2,1,0:T(8,128)(2,1)}), bf16[32,384,128]{2,1,0:T(8,128)(2,1)S(1)}, u32[]{:S(2)}, u32[]{:S(2)}) async-start(bf16[32,384,128]{2,1,0:T(8,128)(2,1)} %bitcast.37), calls=%async_computation.1 | async-start | bytes 6291456 | tf_op jit(solution)/shard_map/all_to_all | solution.py:29
  110.9 104.5 %all-gather.11.cloned.1.call-done = bf16[1,12288,128]{2,1,0:T(8,128)(2,1)} async-done(((bf16[1,1536,128]{2,1,0:T(8,128)(2,1)}), bf16[1,12288,128]{2,1,0:T(8,128)(2,1)}) %all-gather.11.cloned.1.call-update) | async-done | bytes 3145744 | tf_op jit(solution)/shard_map/all_gather | solution.py:28
  215.4 9.6 %all-to-all-done.1 = bf16[32,384,128]{2,1,0:T(8,128)(2,1)S(1)} async-done(((bf16[32,384,128]{2,1,0:T(8,128)(2,1)}), bf16[32,384,128]{2,1,0:T(8,128)(2,1)S(1)}, u32[]{:S(2)}, u32[]{:S(2)}) %all-to-all-start.1) | async-done | bytes 3145760 | tf_op jit(solution)/shard_map/all_to_all | solution.py:29
  225.0 0.0 copy-start
  225.0 5.8 %all-to-all-start = ((bf16[32,384,128]{2,1,0:T(8,128)(2,1)}), bf16[32,384,128]{2,1,0:T(8,128)(2,1)}, u32[]{:S(2)}, u32[]{:S(2)}) async-start(bf16[32,384,128]{2,1,0:T(8,128)(2,1)} %bitcast.36), calls=%async_computation | async-start | bytes 6291456 | tf_op jit(solution)/shard_map/all_to_all | solution.py:29
  230.8 0.0 copy-done
  230.8 0.1 broadcast_bitcast_fusion
  230.9 1.7 broadcast_in_dim.12
  232.6 3.1 copy.8
  235.7 2.8 copy.7
  238.5 95.2 %all-to-all-done = bf16[32,384,128]{2,1,0:T(8,128)(2,1)} async-done(((bf16[32,384,128]{2,1,0:T(8,128)(2,1)}), bf16[32,384,128]{2,1,0:T(8,128)(2,1)}, u32[]{:S(2)}, u32[]{:S(2)}) %all-to-all-start) | async-done | bytes 3145760 | tf_op jit(solution)/shard_map/all_to_all | solution.py:29
  333.7 3.4 copy.6
  337.1 37.2 %all-gather.13.cloned.1.call-done = bf16[1,1536,4096]{2,1,0:T(8,128)(2,1)} async-done(((bf16[1,1536,128]{2,1,0:T(8,128)(2,1)}), bf16[1,1536,4096]{2,1,0:T(8,128)(2,1)}) %all-gather.13.cloned.1.call-update) | async-done | bytes 12582928 | tf_op jit(solution)/shard_map/all_gather | solution.py:31
  374.3 11.6 %fusion = f32[1536,384]{1,0:T(8,128)} fusion(bf16[384,4096]{0,1:T(8,128)(2,1)} %bitcast.39, bf16[1,1536,4096]{2,1,0:T(8,128)(2,1)} %all-gather.13.cloned.1.call-done), kind=kOutput, calls=%fused_computation | convolution fusion | flops 4831838208 | bytes 18087936 | tf_op jit(solution)/shard_map/dot_general | solution.py:16
  386.0 94.7 %all-gather.9.cloned.1.call-done = bf16[1,1536,4096]{2,1,0:T(8,128)(2,1)} async-done(((bf16[1,1536,128]{2,1,0:T(8,128)(2,1)}), bf16[1,1536,4096]{2,1,0:T(8,128)(2,1)}) %all-gather.9.cloned.1.call-update) | async-done | bytes 12582928 | tf_op jit(solution)/shard_map/all_gather | solution.py:31
  480.6 11.3 %fusion.7 = f32[1536,384]{1,0:T(8,128)} fusion(f32[1536,384]{1,0:T(8,128)} %copy.8, f32[1536,384]{1,0:T(8,128)} %fusion, bf16[384,4096]{0,1:T(8,128)(2,1)S(1)} %bitcast.38, bf16[1,1536,4096]{2,1,0:T(8,128)(2,1)} %all-gather.9.cloned.1.call-done), kind=kOutput, calls=%fused_computation.5 | convolution fusion | flops 4833017856 | bytes 22806528 | tf_op jit(solution)/shard_map/dot_general | solution.py:16
  (4 shorter events, 0.0 us)
Async XLA Ops:
  6.5 98.8 %all-gather.15.cloned.1.call-start = ((), (), s32[]{:S(2)}) async-start(), calls=%async_computation.5 | async-start | bytes 3538944 | tf_op jit(solution)/shard_map/all_gather | solution.py:28
  9.9 205.5 %all-gather.11.cloned.1.call-start = ((), (), s32[]{:S(2)}) async-start(), calls=%async_computation.3 | async-start | bytes 3538944 | tf_op jit(solution)/shard_map/all_gather | solution.py:28
  10.7 363.7 %all-gather.13.cloned.1.call-start = ((), (), s32[]{:S(2)}) async-start(), calls=%async_computation.4 | async-start | bytes 12976128 | tf_op jit(solution)/shard_map/all_gather | solution.py:31
  11.4 469.3 %all-gather.9.cloned.1.call-start = ((), (), s32[]{:S(2)}) async-start(), calls=%async_computation.2 | async-start | bytes 12976128 | tf_op jit(solution)/shard_map/all_gather | solution.py:31
  105.3 119.7 %all-to-all-start.1 = ((bf16[32,384,128]{2,1,0:T(8,128)(2,1)}), bf16[32,384,128]{2,1,0:T(8,128)(2,1)S(1)}, u32[]{:S(2)}, u32[]{:S(2)}) async-start(bf16[32,384,128]{2,1,0:T(8,128)(2,1)} %bitcast.37), calls=%async_computation.1 | async-start | bytes 6291456 | tf_op jit(solution)/shard_map/all_to_all | solution.py:29
  225.0 5.8 %copy-start = (s32[12,3]{0,1:T(4,128)S(1)}, s32[12,3]{0,1:T(4,128)}, u32[]{:S(2)}) copy-start(s32[12,3]{0,1:T(4,128)} %param.5) | copy-start | bytes 436
  225.0 108.7 %all-to-all-start = ((bf16[32,384,128]{2,1,0:T(8,128)(2,1)}), bf16[32,384,128]{2,1,0:T(8,128)(2,1)}, u32[]{:S(2)}, u32[]{:S(2)}) async-start(bf16[32,384,128]{2,1,0:T(8,128)(2,1)} %bitcast.36), calls=%async_computation | async-start | bytes 6291456 | tf_op jit(solution)/shard_map/all_to_all | solution.py:29
Sparse Core Ops, SparseCore 0:
  10.0 95.2 all-gather.14
  107.9 107.4 all-gather.10
  217.2 157.1 all-gather.12
  376.0 104.6 all-gather.8
where the time goes:
time: 499 us
  waiting for transfers between devices  437 us (88%)
  matrix products  23 us (5%)
  between operations  13.2 us (3%)
  local copies, waits for them, and re-layouts  12.1 us (2%)
  starting transfers between devices  11.5 us (2%)
    all_gather x2, waiting for transfers between devices, shards(): all_pages = lax.all_gather(local_panel, 'row', axis=0, tiled=True)  198 us
    all_gather x2, waiting for transfers between devices, shards(): lax.all_gather(local_panel, 'col', axis=1, tiled=True)  132 us
    all_to_all x2, waiting for transfers between devices, shards(): lax.all_to_all(all_pages, 'col', split_axis=0, concat_axis=1, tiled=True)  105 us
    dot_general x2, matrix products, product_nt(): lax.dot_general(left, right, (((1,), (1,)), ((), ())), preferred_element_...  23 us
    all_to_all x2, starting transfers between devices, shards(): lax.all_to_all(all_pages, 'col', split_axis=0, concat_axis=1, tiled=True)  11.3 us
  transfers between devices with their start and end apart: 6, of which 6 were waited for; matrix products, arithmetic and copies ran while one was open for 5% of the time, Pallas kernels for 0%

commit v1 on v0

--- a/solution.py
+++ b/solution.py
@@ -28,7 +28,10 @@
         all_pages = lax.all_gather(local_panel, "row", axis=0, tiled=True)
         column_block = lax.all_to_all(all_pages, "col", split_axis=0, concat_axis=1, tiled=True)
         total = total + product_nt(
-            lax.all_gather(local_panel, "col", axis=1, tiled=True), column_block
+            jnp.concatenate(
+                lax.all_to_all(jnp.stack([local_panel] * lax.axis_size("col")), "col", 0, 0), axis=1
+            ),
+            column_block,
         )
     return total * spread_tiles(c_mask).astype(jnp.float32)
 

time: 499 us -> 897 us (1.80)
  blocking collectives: 0 us -> 359 us
  waiting for transfers between devices: 437 us -> 470 us
    all_to_all x0 -> x2, blocking collectives: none -> 359 us  [the longest x1 280 us: shards(): lax.all_to_all(jnp.stack([local_panel] * lax.axis_size('col')), 'col', 0, 0)]
    all_to_all x0 -> x1, waiting for transfers between devices: none -> 260 us  [shards(): lax.all_to_all(jnp.stack([local_panel] * lax.axis_size('col')), 'col', 0, 0)]
    all_gather x2 -> x0, waiting for transfers between devices: 132 us -> none  [shards(): lax.all_gather(local_panel, 'col', axis=1, tiled=True)]
    all_to_all x2 -> x1, waiting for transfers between devices: 105 us -> 9.64 us  [shards(): lax.all_to_all(all_pages, 'col', split_axis=0, concat_axis=1, tiled=True)]
    another operation x0 -> x2, local copies, waits for them, and re-layouts: none -> 14.8 us  [shards(): jnp.stack([local_panel] * lax.axis_size('col'))]
  transfers between devices with their start and end apart: 6 -> 4, of which waited for: 6 -> 4; matrix products, arithmetic and copies ran while one was open for 5% -> 2% of each run, Pallas kernels for 0% -> 0%
where the time goes in v1:
time: 897 us
  waiting for transfers between devices  470 us (52%)
  blocking collectives  359 us (40%)
  matrix products  23.1 us (3%)
  local copies, waits for them, and re-layouts  18.3 us (2%)
  between operations  13.5 us (2%)
  starting transfers between devices  10.7 us (1%)
    all_to_all x1, blocking collectives, shards(): lax.all_to_all(jnp.stack([local_panel] * lax.axis_size('col')), 'col', 0, 0)  280 us
    all_to_all x1, waiting for transfers between devices, shards(): lax.all_to_all(jnp.stack([local_panel] * lax.axis_size('col')), 'col', 0, 0)  260 us
    all_gather x2, waiting for transfers between devices, shards(): all_pages = lax.all_gather(local_panel, 'row', axis=0, tiled=True)  199 us
    all_to_all x1, blocking collectives, shards(): lax.all_to_all(all_pages, 'col', split_axis=0, concat_axis=1, tiled=True)  78.7 us
    dot_general x2, matrix products, product_nt(): lax.dot_general(left, right, (((1,), (1,)), ((), ())), preferred_element_...  23.1 us
  transfers between devices with their start and end apart: 4, of which 4 were waited for; matrix products, arithmetic and copies ran while one was open for 2% of the time, Pallas kernels for 0%

profile of v1, /device:TPU:1, one launch (start us, length us, event | category | flops | bytes accessed | tf_op | source)
XLA Modules:
  0.0 896.6 jit_solution(12164170579112518557)
XLA Ops:
  6.5 0.0 all-gather.7.cloned.1.call-start
  6.5 0.7 convert_element_type.22
  7.2 0.1 broadcast_bitcast_fusion.1
  7.3 1.6 broadcast_multiply_fusion
  8.9 1.1 slice_bitcast_fusion.1
  10.0 0.0 all-gather.7.cloned.1.call-update
  10.1 95.4 %all-gather.7.cloned.1.call-done = bf16[1,12288,128]{2,1,0:T(8,128)(2,1)} async-done(((bf16[1,1536,128]{2,1,0:T(8,128)(2,1)}), bf16[1,12288,128]{2,1,0:T(8,128)(2,1)}) %all-gather.7.cloned.1.call-update) | async-done | bytes 3145744 | tf_op jit(solution)/shard_map/all_gather | solution.py:28
  105.5 5.6 all-to-all-start.3
  111.0 0.0 all-gather.5.cloned.1.call-start
  111.1 0.7 all-gather.5.cloned.1.call-update
  111.8 103.8 %all-gather.5.cloned.1.call-done = bf16[1,12288,128]{2,1,0:T(8,128)(2,1)} async-done(((bf16[1,1536,128]{2,1,0:T(8,128)(2,1)}), bf16[1,12288,128]{2,1,0:T(8,128)(2,1)}) %all-gather.5.cloned.1.call-update) | async-done | bytes 3145744 | tf_op jit(solution)/shard_map/all_gather | solution.py:28
  215.6 9.6 %all-to-all-done.3 = bf16[32,384,128]{2,1,0:T(8,128)(2,1)S(1)} async-done(((bf16[32,384,128]{2,1,0:T(8,128)(2,1)}), bf16[32,384,128]{2,1,0:T(8,128)(2,1)S(1)}, u32[]{:S(2)}, u32[]{:S(2)}) %all-to-all-start.3) | async-done | bytes 3145760 | tf_op jit(solution)/shard_map/all_to_all | solution.py:29
  225.2 0.0 copy-start
  225.2 0.0 copy-start.2
  225.2 78.7 %all_to_all.42 = bf16[32,384,128]{2,1,0:T(8,128)(2,1)} all-to-all(bf16[32,384,128]{2,1,0:T(8,128)(2,1)} %bitcast.60), channel_id=1, replica_groups=mesh['row'=8,'col'=32] {'col'}, dimensions={0} | all-to-all | bytes 6291456 | tf_op jit(solution)/shard_map/all_to_all | solution.py:29
  303.9 0.0 copy-done
  303.9 0.0 copy-done.2
  303.9 7.4 stack.7
  311.3 280.2 %all_to_all.43 = bf16[32,1536,128]{2,1,0:T(8,128)(2,1)} all-to-all(bf16[32,1536,128]{2,1,0:T(8,128)(2,1)} %stack.7), channel_id=1, replica_groups=mesh['row'=8,'col'=32] {'col'}, dimensions={0} | all-to-all | bytes 25165824 | tf_op jit(solution)/shard_map/all_to_all | solution.py:32
  591.5 7.4 stack.6
  598.9 0.0 copy-start.3
  598.9 5.1 all-to-all-start
  604.0 0.0 copy-done.3
  604.0 0.1 broadcast_bitcast_fusion
  604.1 0.3 broadcast_in_dim.12
  604.4 2.0 copy.5
  606.3 0.0 copy-start.1
  606.3 11.7 %fusion.21 = f32[1536,384]{1,0:T(8,128)} fusion(bf16[32,384,128]{2,1,0:T(8,128)(2,1)} %copy-done, bf16[32,1536,128]{2,1,0:T(8,128)(2,1)} %all_to_all.43), kind=kOutput, calls=%fused_computation.9 | convolution fusion | flops 4831838208 | bytes 18087936 | tf_op jit(solution)/shard_map/dot_general | solution.py:16
  618.1 260.3 %all-to-all-done = bf16[32,1536,128]{2,1,0:T(8,128)(2,1)} async-done(((bf16[32,1536,128]{2,1,0:T(8,128)(2,1)}), bf16[32,1536,128]{2,1,0:T(8,128)(2,1)}, u32[]{:S(2)}, u32[]{:S(2)}) %all-to-all-start) | async-done | bytes 12582944 | tf_op jit(solution)/shard_map/all_to_all | solution.py:32
  878.4 0.0 copy-done.1
  878.4 11.4 %fusion.16 = f32[1536,384]{1,0:T(8,128)} fusion(f32[1536,384]{1,0:T(8,128)} %copy.5, f32[1536,384]{1,0:T(8,128)} %fusion.21, bf16[32,384,128]{2,1,0:T(8,128)(2,1)S(1)} %copy-done.1, bf16[32,1536,128]{2,1,0:T(8,128)(2,1)} %all-to-all-done), kind=kOutput, calls=%fused_computation.8 | convolution fusion | flops 4833017856 | bytes 22806528 | tf_op jit(solution)/shard_map/dot_general | solution.py:16
  (4 shorter events, 0.0 us)
Async XLA Ops:
  6.5 98.9 %all-gather.7.cloned.1.call-start = ((), (), s32[]{:S(2)}) async-start(), calls=%async_computation.5 | async-start | bytes 3538944 | tf_op jit(solution)/shard_map/all_gather | solution.py:28
  105.5 119.7 %all-to-all-start.3 = ((bf16[32,384,128]{2,1,0:T(8,128)(2,1)}), bf16[32,384,128]{2,1,0:T(8,128)(2,1)S(1)}, u32[]{:S(2)}, u32[]{:S(2)}) async-start(bf16[32,384,128]{2,1,0:T(8,128)(2,1)} %bitcast.59), calls=%async_computation.3 | async-start | bytes 6291456 | tf_op jit(solution)/shard_map/all_to_all | solution.py:29
  111.0 104.5 %all-gather.5.cloned.1.call-start = ((), (), s32[]{:S(2)}) async-start(), calls=%async_computation.4 | async-start | bytes 3538944 | tf_op jit(solution)/shard_map/all_gather | solution.py:28
  225.2 78.7 %copy-start = (bf16[32,384,128]{2,1,0:T(8,128)(2,1)}, bf16[32,384,128]{2,1,0:T(8,128)(2,1)S(1)}, u32[]{:S(2)}) copy-start(bf16[32,384,128]{2,1,0:T(8,128)(2,1)S(1)} %all-to-all-done.3) | copy-start | bytes 9437188
  225.2 78.7 %copy-start.2 = (bf16[1536,128]{1,0:T(8,128)(2,1)S(1)}, bf16[1536,128]{1,0:T(8,128)(2,1)}, u32[]{:S(2)}) copy-start(bf16[1536,128]{1,0:T(8,128)(2,1)} %get-tuple-element.6) | copy-start | bytes 1179652
  598.9 5.1 copy-start.3
  598.9 279.4 %all-to-all-start = ((bf16[32,1536,128]{2,1,0:T(8,128)(2,1)}), bf16[32,1536,128]{2,1,0:T(8,128)(2,1)}, u32[]{:S(2)}, u32[]{:S(2)}) async-start(bf16[32,1536,128]{2,1,0:T(8,128)(2,1)} %stack.6), calls=%async_computation | async-start | bytes 25165824 | tf_op jit(solution)/shard_map/all_to_all | solution.py:32
  606.3 272.0 %copy-start.1 = (bf16[32,384,128]{2,1,0:T(8,128)(2,1)S(1)}, bf16[32,384,128]{2,1,0:T(8,128)(2,1)}, u32[]{:S(2)}) copy-start(bf16[32,384,128]{2,1,0:T(8,128)(2,1)} %all_to_all.42) | copy-start | bytes 9437188
Sparse Core Ops, SparseCore 0:
  10.2 95.2 all-gather.6
  114.5 101.0 all-gather.4

commit v2 on v0

--- a/solution.py
+++ b/solution.py
@@ -26,7 +26,12 @@
     for section in range(SECTIONS):
         local_panel = live_tiles[section]
         all_pages = lax.all_gather(local_panel, "row", axis=0, tiled=True)
-        column_block = lax.all_to_all(all_pages, "col", split_axis=0, concat_axis=1, tiled=True)
+        column_block = jnp.concatenate(
+            lax.all_to_all(
+                jnp.stack(jnp.split(all_pages, lax.axis_size("col"), axis=0)), "col", 0, 0
+            ),
+            axis=1,
+        )
         total = total + product_nt(
             lax.all_gather(local_panel, "col", axis=1, tiled=True), column_block
         )

time: 499 us -> 482 us (0.966)
  waiting for transfers between devices: 437 us -> 345 us
  local copies, waits for them, and re-layouts: 12.1 us -> 87.6 us
    unnamed x7 -> x72, local copies, waits for them, and re-layouts: 0.18 us -> 79.4 us
    all_gather x2, waiting for transfers between devices: 198 us -> 129 us  [shards(): all_pages = lax.all_gather(local_panel, 'row', axis=0, tiled=True)]
    all_to_all x2, waiting for transfers between devices: 105 us -> 42.3 us  [shards(): lax.all_to_all(jnp.stack(jnp.split(all_pages, lax.axis_size('col'), axis=...]
    all_gather x2, waiting for transfers between devices: 132 us -> 172 us  [shards(): lax.all_gather(local_panel, 'col', axis=1, tiled=True)]
    all_to_all x2 -> x0, local copies, waits for them, and re-layouts: 6.22 us -> none  [shards(): lax.all_to_all(all_pages, 'col', split_axis=0, concat_axis=1, tiled=True)]
  transfers between devices with their start and end apart: 6 -> 6, of which waited for: 6 -> 5; matrix products, arithmetic and copies ran while one was open for 5% -> 20% of each run, Pallas kernels for 0% -> 0%
where the time goes in v2:
time: 482 us; the launch traced here: 480 us
  waiting for transfers between devices  345 us (72%)
  local copies, waits for them, and re-layouts  87.6 us (18%)
  matrix products  23.2 us (5%)
  between operations  13.3 us (3%)
  starting transfers between devices  9.73 us (2%)
    all_gather x2, waiting for transfers between devices, shards(): lax.all_gather(local_panel, 'col', axis=1, tiled=True)  172 us
    all_gather x2, waiting for transfers between devices, shards(): all_pages = lax.all_gather(local_panel, 'row', axis=0, tiled=True)  129 us
    unnamed x72, local copies, waits for them, and re-layouts  79.4 us
    all_to_all x2, waiting for transfers between devices, shards(): lax.all_to_all(jnp.stack(jnp.split(all_pages, lax.axis_size('col'), axis=...  42.3 us
    dot_general x2, matrix products, product_nt(): lax.dot_general(left, right, (((1,), (1,)), ((), ())), preferred_element_...  23.2 us
  transfers between devices with their start and end apart: 6, of which 5 were waited for; matrix products, arithmetic and copies ran while one was open for 20% of the time, Pallas kernels for 0%

profile of v2, /device:TPU:1, one launch (start us, length us, event | category | flops | bytes accessed | tf_op | source)
XLA Modules:
  0.0 479.8 jit_solution(8604872485648082257)
XLA Ops:
  6.5 1.4 copy.5
  8.8 1.0 fusion.10
  11.8 93.4 %all-gather.15.cloned.1.call-done = bf16[1,12288,128]{1,2,0:T(8,128)(2,1)} async-done(((bf16[1,1536,128]{1,2,0:T(8,128)(2,1)}), bf16[1,12288,128]{1,2,0:T(8,128)(2,1)}) %all-gather.15.cloned.1.call-update) | async-done | bytes 3145744 | tf_op jit(solution)/shard_map/all_gather | solution.py:28
  105.2 1.5 constant_dynamic-update-slice_fusion.63
  106.8 1.5 constant_dynamic-update-slice_fusion.62
  108.3 1.5 constant_dynamic-update-slice_fusion.61
  109.8 1.5 constant_dynamic-update-slice_fusion.60
  111.4 1.5 constant_dynamic-update-slice_fusion.59
  112.9 1.5 constant_dynamic-update-slice_fusion.58
  114.5 1.6 constant_dynamic-update-slice_fusion.57
  116.0 1.6 constant_dynamic-update-slice_fusion.56
  117.6 1.5 constant_dynamic-update-slice_fusion.55
  119.1 1.5 constant_dynamic-update-slice_fusion.54
  120.7 1.5 constant_dynamic-update-slice_fusion.53
  122.2 1.5 constant_dynamic-update-slice_fusion.52
  123.7 1.5 constant_dynamic-update-slice_fusion.51
  125.3 1.5 constant_dynamic-update-slice_fusion.50
  126.8 1.6 constant_dynamic-update-slice_fusion.49
  128.4 1.5 constant_dynamic-update-slice_fusion.48
  129.9 1.5 constant_dynamic-update-slice_fusion.47
  131.4 1.5 constant_dynamic-update-slice_fusion.46
  133.0 1.5 constant_dynamic-update-slice_fusion.45
  134.5 1.5 constant_dynamic-update-slice_fusion.44
  136.1 1.6 constant_dynamic-update-slice_fusion.43
  137.6 1.5 constant_dynamic-update-slice_fusion.42
  139.1 1.5 constant_dynamic-update-slice_fusion.41
  140.7 1.5 constant_dynamic-update-slice_fusion.40
  142.2 1.5 constant_dynamic-update-slice_fusion.39
  143.7 1.5 constant_dynamic-update-slice_fusion.38
  145.3 1.6 constant_dynamic-update-slice_fusion.37
  146.9 1.6 constant_dynamic-update-slice_fusion.36
  148.4 1.5 constant_dynamic-update-slice_fusion.35
  150.0 1.5 constant_dynamic-update-slice_fusion.34
  151.5 1.5 constant_dynamic-update-slice_fusion.33
  153.1 1.5 constant_dynamic-update-slice_fusion.32
  154.6 5.6 %all-to-all-start.1 = ((bf16[32,384,128]{1,2,0:T(8,128)(2,1)}), bf16[32,384,128]{1,2,0:T(8,128)(2,1)}, u32[]{:S(2)}, u32[]{:S(2)}) async-start(bf16[32,384,128]{1,2,0:T(8,128)(2,1)} %constant_dynamic-update-slice_fusion.32), calls=%async_computation.1 | async-start | bytes 6291456 | tf_op jit(solution)/shard_map/all_to_all | solution.py:30
  160.2 35.2 %all-gather.11.cloned.1.call-done = bf16[1,12288,128]{1,2,0:T(8,128)(2,1)} async-done(((bf16[1,1536,128]{1,2,0:T(8,128)(2,1)}), bf16[1,12288,128]{1,2,0:T(8,128)(2,1)}) %all-gather.11.cloned.1.call-update) | async-done | bytes 3145744 | tf_op jit(solution)/shard_map/all_gather | solution.py:28
  196.3 0.9 constant_dynamic-update-slice_fusion.30
  197.2 0.9 constant_dynamic-update-slice_fusion.29
  224.6 1.7 copy-done
  226.4 42.3 %all-to-all-done.1 = bf16[32,384,128]{1,2,0:T(8,128)(2,1)} async-done(((bf16[32,384,128]{1,2,0:T(8,128)(2,1)}), bf16[32,384,128]{1,2,0:T(8,128)(2,1)}, u32[]{:S(2)}, u32[]{:S(2)}) %all-to-all-start.1) | async-done | bytes 3145760 | tf_op jit(solution)/shard_map/all_to_all | solution.py:30
  268.6 4.0 all-to-all-start
  272.8 1.7 broadcast_in_dim.12
  274.5 3.1 copy.6
  277.6 104.7 %all-gather.13.cloned.1.call-done = bf16[1,1536,4096]{1,2,0:T(8,128)(2,1)} async-done(((bf16[1,1536,128]{1,2,0:T(8,128)(2,1)}), bf16[1,1536,4096]{1,2,0:T(8,128)(2,1)}) %all-gather.13.cloned.1.call-update) | async-done | bytes 12582928 | tf_op jit(solution)/shard_map/all_gather | solution.py:36
  382.2 11.7 %fusion = f32[1536,384]{1,0:T(8,128)} fusion(bf16[384,4096]{0,1:T(8,128)(2,1)} %bitcast.5, bf16[1,1536,4096]{1,2,0:T(8,128)(2,1)} %all-gather.13.cloned.1.call-done), kind=kOutput, calls=%fused_computation | convolution fusion | flops 4831838208 | bytes 18087936 | tf_op jit(solution)/shard_map/dot_general | solution.py:16
  393.9 67.8 %all-gather.9.cloned.1.call-done = bf16[1,1536,4096]{1,2,0:T(8,128)(2,1)} async-done(((bf16[1,1536,128]{1,2,0:T(8,128)(2,1)}), bf16[1,1536,4096]{1,2,0:T(8,128)(2,1)}) %all-gather.9.cloned.1.call-update) | async-done | bytes 12582928 | tf_op jit(solution)/shard_map/all_gather | solution.py:36
  461.8 11.5 %fusion.7 = f32[1536,384]{1,0:T(8,128)} fusion(f32[1536,384]{1,0:T(8,128)} %copy.6, f32[1536,384]{1,0:T(8,128)} %fusion, bf16[384,4096]{0,1:T(8,128)(2,1)S(1)} %bitcast.34, bf16[1,1536,4096]{1,2,0:T(8,128)(2,1)} %all-gather.9.cloned.1.call-done), kind=kOutput, calls=%fused_computation.5 | convolution fusion | flops 4833017856 | bytes 22806528 | tf_op jit(solution)/shard_map/dot_general | solution.py:16
  (50 shorter events, 30.3 us)
Async XLA Ops:
  6.5 98.7 %all-gather.15.cloned.1.call-start = ((), (), s32[]{:S(2)}) async-start(), calls=%async_computation.5 | async-start | bytes 3538944 | tf_op jit(solution)/shard_map/all_gather | solution.py:28
  9.8 185.6 %all-gather.11.cloned.1.call-start = ((), (), s32[]{:S(2)}) async-start(), calls=%async_computation.3 | async-start | bytes 3538944 | tf_op jit(solution)/shard_map/all_gather | solution.py:28
  10.5 371.7 %all-gather.13.cloned.1.call-start = ((), (), s32[]{:S(2)}) async-start(), calls=%async_computation.4 | async-start | bytes 12976128 | tf_op jit(solution)/shard_map/all_gather | solution.py:36
  11.3 450.5 %all-gather.9.cloned.1.call-start = ((), (), s32[]{:S(2)}) async-start(), calls=%async_computation.2 | async-start | bytes 12976128 | tf_op jit(solution)/shard_map/all_gather | solution.py:36
  154.6 114.0 %all-to-all-start.1 = ((bf16[32,384,128]{1,2,0:T(8,128)(2,1)}), bf16[32,384,128]{1,2,0:T(8,128)(2,1)}, u32[]{:S(2)}, u32[]{:S(2)}) async-start(bf16[32,384,128]{1,2,0:T(8,128)(2,1)} %constant_dynamic-update-slice_fusion.32), calls=%async_computation.1 | async-start | bytes 6291456 | tf_op jit(solution)/shard_map/all_to_all | solution.py:30
  224.6 1.7 copy-start
  226.4 46.3 %copy-start.1 = (s32[12,3]{0,1:T(4,128)S(1)}, s32[12,3]{0,1:T(4,128)}, u32[]{:S(2)}) copy-start(s32[12,3]{0,1:T(4,128)} %param.5) | copy-start | bytes 436
  268.6 125.3 %all-to-all-start = ((bf16[32,384,128]{1,2,0:T(8,128)(2,1)}), bf16[32,384,128]{1,2,0:T(8,128)(2,1)S(1)}, u32[]{:S(2)}, u32[]{:S(2)}) async-start(bf16[32,384,128]{1,2,0:T(8,128)(2,1)} %copy-done), calls=%async_computation | async-start | bytes 6291456 | tf_op jit(solution)/shard_map/all_to_all | solution.py:30
Sparse Core Ops, SparseCore 0:
  10.0 95.1 all-gather.14
  107.8 87.5 all-gather.10
  197.3 184.9 all-gather.12
  383.9 77.7 all-gather.8
